TPU v7x, 32 devices: a whole 2x2x4 slice. The times are simulated.
32 devices in a mesh: group: 4 (over y, core), member: 8 (over z, x).
Axes of the slice: x: 2, y: 2, z: 4, core: 2. Of those that a mesh axis runs over, the one named last changes fastest.
Arguments:
- queries: bfloat16 [256, 32, 128], P('group'), may hold values from -0.5 to 0.5
- centroids: bfloat16 [131072, 128], P('member'), may hold values from -0.5 to 0.5
- doc_resid: bfloat16 [8192, 128, 128], P(('group', 'member')), may hold values from -6 to 6
- doc_codes: int32 [8192, 128], P(('group', 'member')), may hold values from 0 to 131071
- doc_scale: bfloat16 [8192], P(('group', 'member')), may hold values from 0.019897461 to 0.19921875
- doc_len: int32 [8192], P(('group', 'member')), may hold values from 1 to 128
- send_list: int32 [32, 32, 2], P(('group', 'member')), may hold values from 0 to 255
- cand: int32 [256, 1024], P('group', 'member'), may hold values from 0 to 63
Outputs:
- scores: float32 [256, 1024], P('group', 'member')
Inputs may be any that keep to these rules, and one draw needn't show every extreme that they name: `cand`: slot s names the document source s div 2 sent to this candidate's device in its slot s mod 2.
All inputs are finite; a program needn't handle non-finite values.
Results may differ from a plain program's by a relative error of at most 0.0003.
Values may be sent and summed in bfloat16 or wider, within the bound.
A program may use at most 256 MiB of HBM per device.

v0:
```python
import functools

import jax
import jax.numpy as jnp
from jax import lax
from jax.experimental import pallas as pl
from jax.experimental.pallas import tpu as pltpu
from jax.sharding import PartitionSpec as P

LANES = 128
PAD = 8
VMEM_LIMIT = 56 * 1024 * 1024


def widen(source, wide, offset, rows):
    step = 256

    @pl.loop(0, rows // step)
    def _(i):
        at = pl.multiple_of(i * step, step)
        wide[pl.ds(at + offset, step), :] = source[pl.ds(at, step), :].astype(jnp.float32)


def fetch_kernel(entries, table, out, wide, stage):
    rows = table.shape[0]
    widen(table, wide, PAD, rows)
    block = stage.shape[0]

    @pl.loop(0, out.shape[0] // block)
    def _(b):
        at = pl.multiple_of(b * block, block)

        @pl.when(entries[at] > 0)
        def _():
            for u in range(block):
                stage[pl.ds(u, 1), :] = wide[pl.ds(entries[at + u], 1), :]
            out[pl.ds(at, block), :] = stage[...].astype(out.dtype)


def fetch_rows(entries, table):
    count, (rows, width) = entries.shape[0], table.shape
    return pl.pallas_call(
        fetch_kernel,
        out_shape=jax.ShapeDtypeStruct((count, width), table.dtype),
        grid_spec=pltpu.PrefetchScalarGridSpec(
            num_scalar_prefetch=1,
            grid=(1,),
            in_specs=[pl.BlockSpec((rows, width), lambda i, e: (0, 0))],
            out_specs=pl.BlockSpec((count, width), lambda i, e: (0, 0)),
            scratch_shapes=[
                pltpu.VMEM((rows + PAD, width), jnp.float32),
                pltpu.VMEM((LANES, width), jnp.float32),
            ],
        ),
        compiler_params=pltpu.CompilerParams(vmem_limit_bytes=VMEM_LIMIT),
    )(entries, table)


def score_kernel(docs, qtokens, chosen, place, lengths, scales, holder, received, *refs):
    residuals, (queries, out, wide, stage, embedded) = refs[:docs], refs[docs:]
    step = pl.program_id(0)
    block, width = stage.shape
    tile = 16

    @pl.when(step == 0)
    def _():
        widen(received, wide, 0, received.shape[0])

    slot = lax.broadcasted_iota(jnp.int32, (block, width), 0)
    for k in range(docs):
        doc = step * docs + k
        length = lengths[doc]
        base = doc * block
        for first in range(0, block, tile):

            @pl.when(first < length)
            def _():
                for u in range(first, first + tile):
                    stage[pl.ds(u, 1), :] = wide[pl.ds(place[base + u], 1), :]

        value = stage[...] + scales[doc] * residuals[k][0].astype(jnp.float32)
        value = jnp.where(slot < length, value, value[0:1, :])
        embedded[pl.ds(k * block, block), :] = value.astype(embedded.dtype)

    chunk = out.shape[1]
    total = jnp.zeros(out.shape, jnp.float32)
    for first in range(0, queries.shape[2], chunk):
        sims = jnp.dot(
            embedded[...],
            queries[0, :, first : first + chunk],
            preferred_element_type=jnp.float32,
        )
        total = total + jnp.max(sims.reshape(docs, block, chunk), axis=1)
    out[...] = total * (1.0 / qtokens)


def score(chosen, place, lengths, scales, holder, received, doc_resid, queries, qcount):
    slots = chosen.shape[0]
    block, width = doc_resid.shape[1:]
    groups, _, columns = queries.shape
    docs = 8
    per_group = slots // groups
    chunk = max(256, qcount)

    def residual_spec(k):
        return pl.BlockSpec(
            (1, block, width), lambda i, chosen, *_: (chosen[i * docs + k], 0, 0)
        )

    out = pl.pallas_call(
        functools.partial(score_kernel, docs, columns // qcount),
        out_shape=jax.ShapeDtypeStruct((slots, chunk), jnp.float32),
        grid_spec=pltpu.PrefetchScalarGridSpec(
            num_scalar_prefetch=5,
            grid=(slots // docs,),
            in_specs=[pl.BlockSpec(received.shape, lambda i, *_: (0, 0))]
            + [residual_spec(k) for k in range(docs)]
            + [
                pl.BlockSpec(
                    (1, width, columns),
                    lambda i, chosen, place, lengths, scales, holder, *_: (
                        holder[i * docs // per_group],
                        0,
                        0,
                    ),
                )
            ],
            out_specs=pl.BlockSpec((docs, chunk), lambda i, *_: (i, 0)),
            scratch_shapes=[
                pltpu.VMEM(received.shape, jnp.float32),
                pltpu.VMEM((block, width), jnp.float32),
                pltpu.VMEM((docs * block, width), jnp.bfloat16),
            ],
        ),
        compiler_params=pltpu.CompilerParams(vmem_limit_bytes=VMEM_LIMIT),
    )(chosen, place, lengths, scales, holder, received, *([doc_resid] * docs), queries)
    return out.reshape(slots, chunk // qcount, qcount).sum(axis=1)


def pack_kernel(members, capacity, codes, place, lists, highest, seen, ranks, sums):
    steps, span = codes.shape
    lines = seen.shape[0]
    part = lines // members
    shard = part * LANES
    stripe = min(256, lines)
    list_lines = lists.shape[0]

    def same(count, row, first=0):
        found = lax.broadcasted_iota(jnp.int32, (count, span), 0) + first == row
        return jnp.where(found, 1.0, 0.0).astype(jnp.bfloat16)

    def across(left, right):
        return lax.dot_general(
            left, right, (((1,), (1,)), ((), ())), preferred_element_type=jnp.float32
        )

    seen[...] = jnp.zeros_like(seen)
    sums[...] = jnp.zeros_like(sums)

    @pl.loop(0, steps)
    def _(i):
        code = codes[pl.ds(i, 1), :]
        line, lane = code >> 7, code & (LANES - 1)
        right = same(LANES, lane)
        for first in range(0, lines, stripe):
            seen[first : first + stripe, :] += across(same(stripe, line, first), right)

    square = (LANES, LANES)
    earlier_lane = lax.broadcasted_iota(jnp.int32, square, 0) < lax.broadcasted_iota(
        jnp.int32, square, 1
    )
    earlier_lane = jnp.where(earlier_lane, 1.0, 0.0).astype(jnp.bfloat16)
    every_lane = jnp.ones(square, jnp.bfloat16)
    square = (part, part)
    earlier_line = lax.broadcasted_iota(jnp.int32, square, 1) < lax.broadcasted_iota(
        jnp.int32, square, 0
    )
    earlier_line = jnp.where(earlier_line, 1.0, 0.0).astype(jnp.bfloat16)
    top = jnp.zeros((1, LANES), jnp.float32)
    for o in range(members):
        at = slice(o * part, (o + 1) * part)
        present = jnp.where(seen[at, :] > 0.0, 1.0, 0.0)
        marks = present.astype(jnp.bfloat16)
        above = jnp.dot(earlier_line, marks, preferred_element_type=jnp.float32)
        rank = jnp.dot(marks, earlier_lane, preferred_element_type=jnp.float32) + jnp.dot(
            above.astype(jnp.bfloat16), every_lane, preferred_element_type=jnp.float32
        )
        top = jnp.maximum(top, jnp.max(present * (rank + 1.0), axis=0, keepdims=True))
        coarse = jnp.floor(rank * (1.0 / LANES))
        fine = rank - coarse * LANES
        ranks[0:LANES, at] = coarse.T.astype(jnp.bfloat16)
        ranks[LANES : 2 * LANES, at] = fine.T.astype(jnp.bfloat16)
    highest[...] = jnp.broadcast_to(top, highest.shape)

    @pl.loop(0, steps)
    def _(i):
        code = codes[pl.ds(i, 1), :]
        line, lane = code >> 7, code & (LANES - 1)
        found = jnp.zeros((2 * LANES, span), jnp.float32)
        for first in range(0, lines, stripe):
            found += jnp.dot(
                ranks[:, first : first + stripe],
                same(stripe, line, first),
                preferred_element_type=jnp.float32,
            )
        mine = lax.broadcasted_iota(jnp.int32, (LANES, span), 0) == lane
        pick = jnp.where(mine, found[:LANES] * LANES + found[LANES:], 0.0)
        rank = jnp.sum(pick, axis=0, keepdims=True).astype(jnp.int32)
        held = (code >= 0) & (rank < capacity)
        owner = jnp.maximum(line, 0) // part
        spot = jnp.where(held, owner * capacity + rank, 0)
        place[pl.ds(i, 1), :] = spot
        entry = code - owner * shard + PAD
        mark = same(list_lines, jnp.where(held, spot >> 7, -1)).astype(jnp.float32)
        left = jnp.concatenate(
            [
                mark * (entry & 255).astype(jnp.float32),
                mark * (entry >> 8).astype(jnp.float32),
                mark,
            ],
            axis=0,
        )
        sums[...] += across(left.astype(jnp.bfloat16), same(LANES, spot & (LANES - 1)))

    times = jnp.maximum(sums[2 * list_lines :, :], 1.0)
    low = (sums[:list_lines, :] / times + 0.5).astype(jnp.int32)
    high = (sums[list_lines : 2 * list_lines, :] / times + 0.5).astype(jnp.int32)
    lists[...] = low + 256 * high


def make_lists(wanted, members, shard, capacity):
    span = 256
    steps = wanted.size // span
    lines = members * shard // LANES
    list_lines = members * capacity // LANES
    place, lists, highest = pl.pallas_call(
        functools.partial(pack_kernel, members, capacity),
        out_shape=(
            jax.ShapeDtypeStruct((steps, span), jnp.int32),
            jax.ShapeDtypeStruct((list_lines, LANES), jnp.int32),
            jax.ShapeDtypeStruct((8, LANES), jnp.float32),
        ),
        scratch_shapes=[
            pltpu.VMEM((lines, LANES), jnp.float32),
            pltpu.VMEM((2 * LANES, lines), jnp.bfloat16),
            pltpu.VMEM((3 * list_lines, LANES), jnp.float32),
        ],
        compiler_params=pltpu.CompilerParams(vmem_limit_bytes=VMEM_LIMIT),
    )(wanted.reshape(steps, span))
    overflow = jnp.max(highest) > capacity
    return lists.reshape(members, capacity), place.reshape(-1), overflow


def around(array, axis):
    size = lax.axis_size(axis)
    return [array] + [
        lax.ppermute(array, axis, [(i, (i + d) % size) for i in range(size)])
        for d in range(1, size)
    ]


def body(queries, centroids, doc_resid, doc_codes, doc_scale, doc_len, send_list, cand):
    groups = lax.axis_size("group")
    members = lax.axis_size("member")
    capacity_sent = send_list.shape[2]
    block, width = doc_resid.shape[1:]
    shard = centroids.shape[0]
    qcount, qtokens = queries.shape[:2]

    chosen = send_list[0].reshape(-1)
    slots = chosen.shape[0]
    codes = jnp.take(doc_codes, chosen, axis=0)
    scales = jnp.take(doc_scale, chosen, axis=0).astype(jnp.float32)
    lengths = jnp.take(doc_len, chosen, axis=0)
    valid = jnp.arange(block, dtype=jnp.int32)[None, :] < lengths[:, None]

    lookups = slots * block
    capacity = -(-lookups // (2 * members * LANES)) * LANES
    lists, place, overflow = make_lists(jnp.where(valid, codes, -1), members, shard, capacity)
    flag = jnp.broadcast_to(overflow.astype(jnp.int32), (members, LANES))
    asked = lax.all_to_all(
        jnp.concatenate([lists, flag], axis=1), "member", split_axis=0, concat_axis=0, tiled=True
    )
    overflow = jnp.max(asked[:, capacity:]) > 0
    rows = fetch_rows(asked[:, :capacity].reshape(-1), centroids)
    received = lax.all_to_all(rows, "member", split_axis=0, concat_axis=0, tiled=True)

    turned = queries.transpose(2, 1, 0).reshape(width, qtokens * qcount)
    every_query = jnp.stack(around(turned, "group"))
    me = lax.axis_index("group")
    holder = lax.rem(me - jnp.arange(groups, dtype=jnp.int32) + groups, groups)

    def listed():
        return score(
            chosen, place, lengths, scales, holder, received, doc_resid, every_query, qcount
        )

    def whole_table():
        copies = jnp.broadcast_to(centroids[None], (members, shard, width))
        table = lax.all_to_all(copies, "member", split_axis=0, concat_axis=0, tiled=True)
        table = table.reshape(members * shard, width)
        base = jnp.take(table, codes.reshape(-1), axis=0)
        own = jnp.arange(lookups, dtype=jnp.int32)
        return score(
            chosen, own, lengths, scales, holder, base, doc_resid, every_query, qcount
        )

    local = lax.cond(overflow, whole_table, listed)
    local = local.reshape(groups * members, capacity_sent, qcount)
    returned = lax.all_to_all(local, ("group", "member"), split_axis=0, concat_axis=0, tiled=True)
    dense = returned.reshape(-1, qcount).T
    hit = cand[:, :, None] == jnp.arange(dense.shape[1], dtype=jnp.int32)
    return jnp.sum(jnp.where(hit, dense[:, None, :], 0.0), axis=2)


def solution(mesh):
    placed = (
        P("group", None, None),
        P("member", None),
        P(("group", "member"), None, None),
        P(("group", "member"), None),
        P(("group", "member")),
        P(("group", "member")),
        P(("group", "member"), None, None),
        P("group", "member"),
    )
    return jax.shard_map(
        body, mesh=mesh, in_specs=placed, out_specs=P("group", "member"), check_vma=False
    )
```

profile of v0, /device:TPU:0, one launch (start us, length us, event | category | flops | bytes accessed | tf_op | source)
XLA Modules:
  0.0 128.9 jit_solution(7135566580255486148)
XLA Ops:
  0.0 0.0 copy-start
  0.0 0.8 copy.34
  0.8 0.1 reshape_squeeze.8
  0.9 0.0 copy-done
  0.9 0.6 gather_fusion.2
  1.6 1.5 %gather_fusion.1 = s32[64]{0:T(128)S(1)} fusion(s32[256]{0:T(256)} %param.15, s32[1024]{0:T(1024)S(1)} %pad_clamp_fusion), kind=kCustom, calls=%fused_computation.1 | custom fusion | bytes 768 | tf_op jit(solution)/shard_map/jit(_take)/gather | solution.py:274
  3.0 0.1 gather.21
  3.1 0.1 copy.35
  3.2 0.7 broadcast_select_fusion.2
  3.9 0.1 copy.36
  4.0 0.1 copy.37
  4.1 0.1 lt.85
  4.2 0.1 broadcast_in_dim.69
  4.3 0.6 select_select_fusion.codes
  4.9 29.1 %shard_map.82 = (s32[32,256]{1,0:T(8,128)S(1)}, s32[32,128]{1,0:T(8,128)}, f32[8,128]{1,0:T(8,128)}) custom-call(s32[32,256]{1,0:T(8,128)} %select_select_fusion.codes), custom_call_target="tpu_custom_call" | custom-call | tf_op jit(solution)/shard_map/pallas_call | solution.py:236
  34.1 0.7 reshape.131
  34.8 1.3 reduce_max.18
  36.8 13.6 %all_to_all.32 = s32[8,1,640]{2,1,0:T(1,128)S(1)} all-to-all(s32[8,1,640]{2,1,0:T(1,128)S(1)} %all_to_all.22), channel_id=1, replica_groups=mesh['group'=4,'member'=8] {'member'}, dimensions={0} | all-to-all | bytes 40960 | tf_op jit(solution)/shard_map/all_to_all | solution.py:281
  50.3 0.6 copy.47
  50.9 7.3 %shard_map.83 = bf16[4096,128]{1,0:T(8,128)(2,1)} custom-call(s32[4096]{0:T(1024)} %bitcast.61, bf16[16384,128]{1,0:T(8,128)(2,1)} %table.1), custom_call_target="tpu_custom_call" | custom-call | tf_op jit(solution)/shard_map/pallas_call | solution.py:42
  58.2 0.0 copy-start.4
  58.2 0.0 copy-start.2
  58.2 3.7 %all-to-all-start.2 = ((bf16[8,512,128]{2,1,0:T(8,128)(2,1)}), bf16[8,512,128]{2,1,0:T(8,128)(2,1)S(1)}, u32[]{:S(2)}, u32[]{:S(2)}) async-start(bf16[8,512,128]{2,1,0:T(8,128)(2,1)} %bitcast.45), calls=%async_computation.2 | async-start | bytes 2097152 | tf_op jit(solution)/shard_map/all_to_all | solution.py:286
  61.9 0.0 copy-done.4
  62.0 0.2 copy.39
  62.2 0.0 copy-start.3
  62.2 0.1 collective-permute-start.2
  62.2 1.6 %collective-permute-start.1 = (bf16[128,2048]{0,1:T(8,128)(2,1)S(1)}, bf16[128,2048]{0,1:T(8,128)(2,1)S(1)}, u32[]{:S(2)}, u32[]{:S(2)}) collective-permute-start(bf16[128,2048]{0,1:T(8,128)(2,1)S(1)} %bitcast.47), channel_id=1, source_target_pairs={{0,16},{8,24},{16,0},{24,8},{1,17},{9,25},{17,1},{25,9},{2,18},{10... | collective-permute-start | bytes 1572872 | tf_op jit(solution)/shard_map/ppermute | solution.py:257
  63.8 0.2 collective-permute-start
  64.0 0.1 reshape_squeeze.9
  64.1 0.0 copy-done.2
  64.1 0.8 gather_fusion.3
  64.9 0.6 slice_reduce_fusion
  66.2 7.3 %collective-permute-done.2 = bf16[128,2048]{0,1:T(8,128)(2,1)S(1)} collective-permute-done((bf16[128,2048]{0,1:T(8,128)(2,1)S(1)}, bf16[128,2048]{0,1:T(8,128)(2,1)S(1)}, u32[]{:S(2)}, u32[]{:S(2)}) %collective-permute-start.2) | collective-permute-done | bytes 524320 | tf_op jit(solution)/shard_map/ppermute | solution.py:257
  73.5 0.0 copy-start.5
  73.5 14.1 %collective-permute-done.1 = bf16[128,2048]{0,1:T(8,128)(2,1)S(1)} collective-permute-done((bf16[128,2048]{0,1:T(8,128)(2,1)S(1)}, bf16[128,2048]{0,1:T(8,128)(2,1)S(1)}, u32[]{:S(2)}, u32[]{:S(2)}) %collective-permute-start.1) | collective-permute-done | bytes 524320 | tf_op jit(solution)/shard_map/ppermute | solution.py:257
  87.6 0.0 copy-start.6
  87.6 0.1 collective-permute-done
  87.7 0.0 copy-start.7
  87.7 0.0 copy-done.3
  87.7 0.0 copy-done.5
  87.7 0.7 copy-done.6
  88.5 0.2 copy-done.7
  88.6 1.8 %pad_maximum_fusion = bf16[4,128,2048]{1,2,0:T(8,128)(2,1)S(1)} fusion(bf16[1,128,2048]{1,2,0:T(8,128)(2,1)} %bitcast.50, bf16[1,128,2048]{1,2,0:T(8,128)(2,1)} %bitcast.51, bf16[1,128,2048]{1,2,0:T(8,128)(2,1)} %bitcast.52, bf16[1,128,2048]{1,2,0:T(8,128)(2,1)} %bitcast.49), kind=kLoop, calls=%fused_computation.10 | loop fusion | flops 3145728 | bytes 4194304 | tf_op jit(solution)/shard_map/stack | solution.py:289
  90.4 0.0 all-to-all-done.2
  90.4 0.0 copy-start.8
  90.4 23.8 %conditional.1 = (f32[64,256]{1,0:T(8,128)S(1)}) conditional(s32[]{:T(128)} %convert_element_type.10, (s32[32,256]{1,0:T(8,128)S(1)}, bf16[8,512,128]{2,1,0:T(8,128)(2,1)S(1)}, s32[64]{0:T(128)S(1)}, s32[64]{0:T(128)S(1)}, f32[64]{0:T(128)S(1)}, /*index=5*/s32[4]{0:T(128)S(1)}, bf16[256,128,128]{2,1,0:T(8,128)(2,1)}, ...), branch_computations={%region_2.3_spmd, %region_3.4_spmd} | conditional | flops 1138688 | bytes 151273568 | solution.py:308
  90.4 0.6 copy.44
  91.1 2.7 %copy.40.refs_8_ = bf16[4,128,2048]{2,1,0:T(8,128)(2,1)} copy(bf16[4,128,2048]{1,2,0:T(8,128)(2,1)S(1)} %get-tuple-element.113) | data formatting | bytes 4194304 | tf_op jit(solution)/shard_map
  93.7 20.5 %branch_0_fun.1 = f32[64,256]{1,0:T(8,128)S(1)} custom-call(s32[64]{0:T(128)S(1)} %get-tuple-element.43.chosen, s32[8192]{0:T(1024)} %bitcast.53, s32[64]{0:T(128)S(1)} %get-tuple-element.45.lengths, f32[64]{0:T(128)S(1)} %get-tuple-element.46.scales, s32[4]{0:T(128)S(1)} %get-tuple-element.47.holder, bf16[4096,128]{1,0:T(8,128)(2,1)S(1)} %bitcast.44, ...), custom_call_target="tpu_custom_call" | custom-call | tf_op jit(solution)/shard_map/cond/branch_0_fun/pallas_call | solution.py:110
  114.2 0.0 copy-start.1
  114.3 0.1 reshape.134
  114.4 0.1 reduce_sum.22
  114.5 0.1 reshape.169
  114.6 11.6 %all_to_all.33 = f32[32,1,128]{2,1,0:T(1,128)S(1)} all-to-all(f32[32,1,128]{2,1,0:T(1,128)S(1)} %reshape.169), channel_id=1, replica_groups=mesh['group'=4,'member'=8] {'group','member'}, dimensions={0} | all-to-all | bytes 32768 | tf_op jit(solution)/shard_map/all_to_all | solution.py:310
  126.2 0.5 broadcast.104
  126.7 0.7 reduce
  127.4 0.1 reshape.170
  127.5 0.1 copy.42
  127.5 0.0 copy-done.8
  127.5 1.3 %select_reduce_fusion = f32[64,128]{1,0:T(8,128)} fusion(f32[64,64]{1,0:T(8,128)S(1)} %copy.42, s32[64,128]{1,0:T(8,128)S(1)} %copy-done.8), kind=kLoop, calls=%fused_computation.11 | loop fusion | flops 1564672 | bytes 81920 | tf_op jit(solution)/shard_map/reduce_sum | solution.py:313
  128.9 0.0 copy-done.1
  (11 shorter events, 0.1 us)
Async XLA Ops:
  0.0 0.9 copy-start
  58.2 3.7 %copy-start.4 = (bf16[64,32,128]{2,1,0:T(8,128)(2,1)S(1)}, bf16[64,32,128]{2,1,0:T(8,128)(2,1)}, u32[]{:S(2)}) copy-start(bf16[64,32,128]{2,1,0:T(8,128)(2,1)} %param.10) | copy-start | bytes 1572868
  58.2 5.8 %copy-start.2 = (bf16[256]{0:T(256)(128)(2,1)S(1)}, bf16[256]{0:T(256)(128)(2,1)}, u32[]{:S(2)}) copy-start(bf16[256]{0:T(256)(128)(2,1)} %param.14) | copy-start | bytes 1540
  58.2 32.2 %all-to-all-start.2 = ((bf16[8,512,128]{2,1,0:T(8,128)(2,1)}), bf16[8,512,128]{2,1,0:T(8,128)(2,1)S(1)}, u32[]{:S(2)}, u32[]{:S(2)}) async-start(bf16[8,512,128]{2,1,0:T(8,128)(2,1)} %bitcast.45), calls=%async_computation.2 | async-start | bytes 2097152 | tf_op jit(solution)/shard_map/all_to_all | solution.py:286
  62.2 25.6 %copy-start.3 = (bf16[64,32,128]{2,0,1:T(8,128)(2,1)}, bf16[64,32,128]{2,0,1:T(8,128)(2,1)S(1)}, u32[]{:S(2)}) copy-start(bf16[64,32,128]{2,0,1:T(8,128)(2,1)S(1)} %copy.39) | copy-start | bytes 1572868
  62.2 11.3 %collective-permute-start.2 = (bf16[128,2048]{0,1:T(8,128)(2,1)S(1)}, bf16[128,2048]{0,1:T(8,128)(2,1)S(1)}, u32[]{:S(2)}, u32[]{:S(2)}) collective-permute-start(bf16[128,2048]{0,1:T(8,128)(2,1)S(1)} %bitcast.46), channel_id=1, source_target_pairs={{0,24},{8,0},{16,8},{24,16},{1,25},{9,1},{17,9},{25,17},{2,26},{10... | collective-permute-start | bytes 1572872 | tf_op jit(solution)/shard_map/ppermute | solution.py:257
  62.2 25.4 %collective-permute-start.1 = (bf16[128,2048]{0,1:T(8,128)(2,1)S(1)}, bf16[128,2048]{0,1:T(8,128)(2,1)S(1)}, u32[]{:S(2)}, u32[]{:S(2)}) collective-permute-start(bf16[128,2048]{0,1:T(8,128)(2,1)S(1)} %bitcast.47), channel_id=1, source_target_pairs={{0,16},{8,24},{16,0},{24,8},{1,17},{9,25},{17,1},{25,9},{2,18},{10... | collective-permute-start | bytes 1572872 | tf_op jit(solution)/shard_map/ppermute | solution.py:257
  63.8 23.9 %collective-permute-start = (bf16[128,2048]{0,1:T(8,128)(2,1)S(1)}, bf16[128,2048]{0,1:T(8,128)(2,1)S(1)}, u32[]{:S(2)}, u32[]{:S(2)}) collective-permute-start(bf16[128,2048]{0,1:T(8,128)(2,1)S(1)} %bitcast.48), channel_id=1, source_target_pairs={{0,8},{8,16},{16,24},{24,0},{1,9},{9,17},{17,25},{25,1},{2,10},{10... | collective-permute-start | bytes 1572872 | tf_op jit(solution)/shard_map/ppermute | solution.py:257
  73.5 14.2 %copy-start.5 = (bf16[128,2048]{0,1:T(8,128)(2,1)}, bf16[128,2048]{0,1:T(8,128)(2,1)S(1)}, u32[]{:S(2)}) copy-start(bf16[128,2048]{0,1:T(8,128)(2,1)S(1)} %collective-permute-done.2) | copy-start | bytes 1572868
  87.6 0.8 copy-start.6
  87.7 0.9 copy-start.7
  90.4 37.1 %copy-start.8 = (s32[64,128]{1,0:T(8,128)S(1)}, s32[64,128]{1,0:T(8,128)}, u32[]{:S(2)}) copy-start(s32[64,128]{1,0:T(8,128)} %param.17) | copy-start | bytes 98308
  114.2 14.6 %copy-start.1 = (s32[256,128]{1,0:T(8,128)S(1)}, s32[256,128]{1,0:T(8,128)}, u32[]{:S(2)}) copy-start(s32[256,128]{1,0:T(8,128)} %param.13) | copy-start | bytes 393220
where the time goes:
time: 130 us; the launch traced here: 129 us
  Pallas kernels  56.9 us (44%)
  blocking collectives  25.2 us (19%)
  waiting for transfers between devices  21.5 us (17%)
  local copies, waits for them, and re-layouts  11.1 us (9%)
  other arithmetic  7.13 us (5%)
  starting transfers between devices  5.47 us (4%)
  between operations  1.53 us (1%)
    pallas_call x1, Pallas kernels, make_lists(): pl.pallas_call(functools.partial(pack_kernel, members, capacity), out_sha...  29.1 us
    ppermute x3, waiting for transfers between devices, around(): lax.ppermute(array, axis, [(i, (i + d) % size) for i in range(size)])  21.5 us
    pallas_call x1, Pallas kernels, score(): pl.pallas_call(functools.partial(score_kernel, docs, columns // qcount),...  20.5 us
    all_to_all x1, blocking collectives, body(): lax.all_to_all(jnp.concatenate([lists, flag], axis=1), 'member', split_ax...  13.6 us
    all_to_all x1, blocking collectives, body(): lax.all_to_all(local, ('group', 'member'), split_axis=0, concat_axis=0, t...  11.6 us
    pallas_call x1, Pallas kernels, fetch_rows(): pl.pallas_call(fetch_kernel, out_shape=jax.ShapeDtypeStruct((count, width...  7.3 us
    all_to_all x1, starting transfers between devices, body(): lax.all_to_all(rows, 'member', split_axis=0, concat_axis=0, tiled=True)  3.69 us
    unnamed x25, local copies, waits for them, and re-layouts  2.73 us
  transfers between devices with their start and end apart: 4, of which 3 were waited for; matrix products, arithmetic and copies ran while one was open for 3% of the time, Pallas kernels for 0%

commit v1 on v0

--- a/solution.py
+++ b/solution.py
@@ -8,6 +8,7 @@
 from jax.sharding import PartitionSpec as P
 
 LANES = 128
+GRAIN = 256
 PAD = 8
 VMEM_LIMIT = 56 * 1024 * 1024
 
@@ -84,10 +85,11 @@
 
     chunk = out.shape[1]
     total = jnp.zeros(out.shape, jnp.float32)
-    for first in range(0, queries.shape[2], chunk):
-        sims = jnp.dot(
+    for first in range(0, queries.shape[1], chunk):
+        sims = lax.dot_general(
             embedded[...],
-            queries[0, :, first : first + chunk],
+            queries[0, first : first + chunk, :],
+            (((1,), (1,)), ((), ())),
             preferred_element_type=jnp.float32,
         )
         total = total + jnp.max(sims.reshape(docs, block, chunk), axis=1)
@@ -97,7 +99,7 @@
 def score(chosen, place, lengths, scales, holder, received, doc_resid, queries, qcount):
     slots = chosen.shape[0]
     block, width = doc_resid.shape[1:]
-    groups, _, columns = queries.shape
+    groups, columns, _ = queries.shape
     docs = 8
     per_group = slots // groups
     chunk = max(256, qcount)
@@ -117,7 +119,7 @@
             + [residual_spec(k) for k in range(docs)]
             + [
                 pl.BlockSpec(
-                    (1, width, columns),
+                    (1, columns, width),
                     lambda i, chosen, place, lengths, scales, holder, *_: (
                         holder[i * docs // per_group],
                         0,
@@ -137,17 +139,22 @@
     return out.reshape(slots, chunk // qcount, qcount).sum(axis=1)
 
 
-def pack_kernel(members, capacity, codes, place, lists, highest, seen, ranks, sums):
+def pack_kernel(members, capacity, codes, place, lists, highest, seen, whole, ranks, sums):
     steps, span = codes.shape
     lines = seen.shape[0]
     part = lines // members
-    shard = part * LANES
+    shard = part * GRAIN
     stripe = min(256, lines)
+    bits = GRAIN.bit_length() - 1
     list_lines = lists.shape[0]
 
     def same(count, row, first=0):
-        found = lax.broadcasted_iota(jnp.int32, (count, span), 0) + first == row
-        return jnp.where(found, 1.0, 0.0).astype(jnp.bfloat16)
+        row = jnp.broadcast_to((row - first).astype(jnp.float32), (16, span))
+        row = row.astype(jnp.bfloat16)[None]
+        index = lax.broadcasted_iota(jnp.int32, (count, span), 0).astype(jnp.float32)
+        index = index.astype(jnp.bfloat16).reshape(count // 16, 16, span)
+        one, zero = jnp.ones((), jnp.bfloat16), jnp.zeros((), jnp.bfloat16)
+        return jnp.where(index == row, one, zero).reshape(count, span)
 
     def across(left, right):
         return lax.dot_general(
@@ -157,15 +164,15 @@
     seen[...] = jnp.zeros_like(seen)
     sums[...] = jnp.zeros_like(sums)
 
-    @pl.loop(0, steps)
+    @pl.loop(0, steps, unroll=4)
     def _(i):
         code = codes[pl.ds(i, 1), :]
-        line, lane = code >> 7, code & (LANES - 1)
-        right = same(LANES, lane)
+        line, lane = code >> bits, code & (GRAIN - 1)
+        right = same(GRAIN, lane)
         for first in range(0, lines, stripe):
             seen[first : first + stripe, :] += across(same(stripe, line, first), right)
 
-    square = (LANES, LANES)
+    square = (GRAIN, GRAIN)
     earlier_lane = lax.broadcasted_iota(jnp.int32, square, 0) < lax.broadcasted_iota(
         jnp.int32, square, 1
     )
@@ -176,7 +183,7 @@
         jnp.int32, square, 0
     )
     earlier_line = jnp.where(earlier_line, 1.0, 0.0).astype(jnp.bfloat16)
-    top = jnp.zeros((1, LANES), jnp.float32)
+    top = jnp.zeros((1, GRAIN), jnp.float32)
     for o in range(members):
         at = slice(o * part, (o + 1) * part)
         present = jnp.where(seen[at, :] > 0.0, 1.0, 0.0)
@@ -188,23 +195,23 @@
         top = jnp.maximum(top, jnp.max(present * (rank + 1.0), axis=0, keepdims=True))
         coarse = jnp.floor(rank * (1.0 / LANES))
         fine = rank - coarse * LANES
-        ranks[0:LANES, at] = coarse.T.astype(jnp.bfloat16)
-        ranks[LANES : 2 * LANES, at] = fine.T.astype(jnp.bfloat16)
+        whole[at, :] = jnp.concatenate([coarse, fine], axis=1)
     highest[...] = jnp.broadcast_to(top, highest.shape)
-
-    @pl.loop(0, steps)
+    ranks[...] = whole[...].T.astype(jnp.bfloat16)
+
+    @pl.loop(0, steps, unroll=4)
     def _(i):
         code = codes[pl.ds(i, 1), :]
-        line, lane = code >> 7, code & (LANES - 1)
-        found = jnp.zeros((2 * LANES, span), jnp.float32)
+        line, lane = code >> bits, code & (GRAIN - 1)
+        found = jnp.zeros((2 * GRAIN, span), jnp.float32)
         for first in range(0, lines, stripe):
             found += jnp.dot(
                 ranks[:, first : first + stripe],
                 same(stripe, line, first),
                 preferred_element_type=jnp.float32,
             )
-        mine = lax.broadcasted_iota(jnp.int32, (LANES, span), 0) == lane
-        pick = jnp.where(mine, found[:LANES] * LANES + found[LANES:], 0.0)
+        mine = lax.broadcasted_iota(jnp.int32, (GRAIN, span), 0) == lane
+        pick = jnp.where(mine, found[:GRAIN] * LANES + found[GRAIN:], 0.0)
         rank = jnp.sum(pick, axis=0, keepdims=True).astype(jnp.int32)
         held = (code >= 0) & (rank < capacity)
         owner = jnp.maximum(line, 0) // part
@@ -231,20 +238,24 @@
 def make_lists(wanted, members, shard, capacity):
     span = 256
     steps = wanted.size // span
-    lines = members * shard // LANES
+    lines = members * shard // GRAIN
     list_lines = members * capacity // LANES
     place, lists, highest = pl.pallas_call(
         functools.partial(pack_kernel, members, capacity),
         out_shape=(
             jax.ShapeDtypeStruct((steps, span), jnp.int32),
             jax.ShapeDtypeStruct((list_lines, LANES), jnp.int32),
-            jax.ShapeDtypeStruct((8, LANES), jnp.float32),
+            jax.ShapeDtypeStruct((8, GRAIN), jnp.float32),
         ),
         scratch_shapes=[
-            pltpu.VMEM((lines, LANES), jnp.float32),
-            pltpu.VMEM((2 * LANES, lines), jnp.bfloat16),
+            pltpu.VMEM((lines, GRAIN), jnp.float32),
+            pltpu.VMEM((lines, 2 * GRAIN), jnp.float32),
+            pltpu.VMEM((2 * GRAIN, lines), jnp.bfloat16),
             pltpu.VMEM((3 * list_lines, LANES), jnp.float32),
         ],
+        cost_estimate=pl.CostEstimate(
+            flops=24 * wanted.size * lines * GRAIN, bytes_accessed=12 * wanted.size, transcendentals=0
+        ),
         compiler_params=pltpu.CompilerParams(vmem_limit_bytes=VMEM_LIMIT),
     )(wanted.reshape(steps, span))
     overflow = jnp.max(highest) > capacity
@@ -267,6 +278,8 @@
     shard = centroids.shape[0]
     qcount, qtokens = queries.shape[:2]
 
+    turned = queries.transpose(1, 0, 2).reshape(qtokens * qcount, width)
+    every_query = jnp.stack(around(turned, "group"))
     chosen = send_list[0].reshape(-1)
     slots = chosen.shape[0]
     codes = jnp.take(doc_codes, chosen, axis=0)
@@ -281,12 +294,11 @@
     asked = lax.all_to_all(
         jnp.concatenate([lists, flag], axis=1), "member", split_axis=0, concat_axis=0, tiled=True
     )
+    asked, every_query = lax.optimization_barrier((asked, every_query))
     overflow = jnp.max(asked[:, capacity:]) > 0
     rows = fetch_rows(asked[:, :capacity].reshape(-1), centroids)
     received = lax.all_to_all(rows, "member", split_axis=0, concat_axis=0, tiled=True)
 
-    turned = queries.transpose(2, 1, 0).reshape(width, qtokens * qcount)
-    every_query = jnp.stack(around(turned, "group"))
     me = lax.axis_index("group")
     holder = lax.rem(me - jnp.arange(groups, dtype=jnp.int32) + groups, groups)
 

time: 130 us -> 116 us (0.89)
  Pallas kernels: 56.9 us -> 43 us
  blocking collectives: 25.2 us -> 22.2 us
  waiting for transfers between devices: 21.5 us -> 24.1 us
  starting transfers between devices: 5.47 us -> 6.95 us
  local copies, waits for them, and re-layouts: 11.1 us -> 9.77 us
    all_to_all x1, waiting for transfers between devices: 0.01 us -> 24.1 us  [body(): lax.all_to_all(rows, 'member', split_axis=0, concat_axis=0, tiled=True)]
    ppermute x3, waiting for transfers between devices: 21.5 us -> 0.01 us  [around(): lax.ppermute(array, axis, [(i, (i + d) % size) for i in range(size)])]
    pallas_call x1, Pallas kernels: 29.1 us -> 18.6 us  [make_lists(): pl.pallas_call(functools.partial(pack_kernel, members, capacity), out_sha...]
    another operation x1 -> x0, local copies, waits for them, and re-layouts: 2.65 us -> none
    pallas_call x1, Pallas kernels: 7.3 us -> 5.01 us  [fetch_rows(): pl.pallas_call(fetch_kernel, out_shape=jax.ShapeDtypeStruct((count, width...]
    all_to_all x1, blocking collectives: 11.6 us -> 9.91 us  [body(): lax.all_to_all(local, ('group', 'member'), split_axis=0, concat_axis=0, t...]
    ppermute x3, starting transfers between devices: 1.78 us -> 3.26 us  [around(): lax.ppermute(array, axis, [(i, (i + d) % size) for i in range(size)])]
    all_to_all x1, blocking collectives: 13.6 us -> 12.3 us  [body(): lax.all_to_all(jnp.concatenate([lists, flag], axis=1), 'member', split_ax...]
  transfers between devices with their start and end apart: 4 -> 4, of which waited for: 3 -> 1; matrix products, arithmetic and copies ran while one was open for 3% -> 7% of each run, Pallas kernels for 0% -> 16%
where the time goes in v1:
time: 116 us; the launch traced here: 115 us
  Pallas kernels  43 us (37%)
  waiting for transfers between devices  24.1 us (21%)
  blocking collectives  22.2 us (19%)
  local copies, waits for them, and re-layouts  9.77 us (8%)
  other arithmetic  6.99 us (6%)
  starting transfers between devices  6.95 us (6%)
  between operations  1.52 us (1%)
    all_to_all x1, waiting for transfers between devices, body(): lax.all_to_all(rows, 'member', split_axis=0, concat_axis=0, tiled=True)  24.1 us
    pallas_call x1, Pallas kernels, score(): pl.pallas_call(functools.partial(score_kernel, docs, columns // qcount),...  19.4 us
    pallas_call x1, Pallas kernels, make_lists(): pl.pallas_call(functools.partial(pack_kernel, members, capacity), out_sha...  18.6 us
    all_to_all x1, blocking collectives, body(): lax.all_to_all(jnp.concatenate([lists, flag], axis=1), 'member', split_ax...  12.3 us
    all_to_all x1, blocking collectives, body(): lax.all_to_all(local, ('group', 'member'), split_axis=0, concat_axis=0, t...  9.91 us
    pallas_call x1, Pallas kernels, fetch_rows(): pl.pallas_call(fetch_kernel, out_shape=jax.ShapeDtypeStruct((count, width...  5.01 us
    all_to_all x1, starting transfers between devices, body(): lax.all_to_all(rows, 'member', split_axis=0, concat_axis=0, tiled=True)  3.69 us
    ppermute x3, starting transfers between devices, around(): lax.ppermute(array, axis, [(i, (i + d) % size) for i in range(size)])  3.26 us
  transfers between devices with their start and end apart: 4, of which 1 were waited for; matrix products, arithmetic and copies ran while one was open for 7% of the time, Pallas kernels for 16%

profile of v1, /device:TPU:0, one launch (start us, length us, event | category | flops | bytes accessed | tf_op | source)
XLA Modules:
  0.0 114.6 jit_solution(2617959109591075040)
XLA Ops:
  0.0 0.0 copy-start
  0.0 1.3 %copy.36 = bf16[32,64,128]{2,1,0:T(8,128)(2,1)S(1)} copy(bf16[32,64,128]{2,0,1:T(8,128)(2,1)} %bitcast.48) | data formatting | bytes 1048576 | tf_op jit(solution)/shard_map/transpose | solution.py:281
  1.3 2.5 %collective-permute-start.2 = (bf16[2048,128]{1,0:T(8,128)(2,1)S(1)}, bf16[2048,128]{1,0:T(8,128)(2,1)S(1)}, u32[]{:S(2)}, u32[]{:S(2)}) collective-permute-start(bf16[2048,128]{1,0:T(8,128)(2,1)S(1)} %bitcast.44), channel_id=1, source_target_pairs={{0,24},{8,0},{16,8},{24,16},{1,25},{9,1},{17,9},{25,17},{2,26},{10... | collective-permute-start | bytes 1572872 | tf_op jit(solution)/shard_map/ppermute | solution.py:268
  3.7 0.6 collective-permute-start.1
  4.4 0.2 collective-permute-start
  4.6 0.8 copy.32
  5.3 0.1 reshape_squeeze.8
  5.4 0.0 copy-done
  5.5 0.6 gather_fusion.2
  6.1 1.5 %gather_fusion.1 = s32[64]{0:T(128)S(1)} fusion(s32[256]{0:T(256)} %param.15, s32[1024]{0:T(1024)S(1)} %pad_clamp_fusion), kind=kCustom, calls=%fused_computation.1 | custom fusion | bytes 768 | tf_op jit(solution)/shard_map/jit(_take)/gather | solution.py:287
  7.5 0.1 gather.21
  7.6 0.1 copy.33
  7.7 0.7 broadcast_select_fusion.2
  8.4 0.1 copy.34
  8.5 0.1 copy.35
  8.6 0.1 lt.85
  8.7 0.1 broadcast_in_dim.69
  8.8 0.6 select_select_fusion.codes
  9.4 18.6 %shard_map.82 = (s32[32,256]{1,0:T(8,128)S(1)}, s32[32,128]{1,0:T(8,128)}, f32[8,256]{1,0:T(8,128)}) custom-call(s32[32,256]{1,0:T(8,128)} %select_select_fusion.codes), custom_call_target="tpu_custom_call" | custom-call | flops 25769803776 | bytes 98304 | tf_op jit(solution)/shard_map/pallas_call | solution.py:243
  28.1 0.7 reshape.131
  28.8 1.3 %reduce_max.18 = f32[]{:T(128)} reduce(f32[8,256]{1,0:T(8,128)} %get-tuple-element.65, f32[]{:T(128)} %constant.73.clone.1), dimensions={0,1}, to_apply=%region_0.1 | reduce | flops 2047 | bytes 8200 | tf_op jit(solution)/shard_map/reduce_max | solution.py:261
  30.8 12.3 %all_to_all.32 = s32[8,1,640]{2,1,0:T(1,128)S(1)} all-to-all(s32[8,1,640]{2,1,0:T(1,128)S(1)} %all_to_all.22), channel_id=1, replica_groups=mesh['group'=4,'member'=8] {'member'}, dimensions={0} | all-to-all | bytes 40960 | tf_op jit(solution)/shard_map/all_to_all | solution.py:294
  43.1 0.0 collective-permute-done.2
  43.1 0.0 collective-permute-done.1
  43.1 0.0 copy-start.4
  43.1 0.0 collective-permute-done
  43.1 0.0 copy-start.5
  43.1 0.8 copy-done.4
  43.9 0.2 copy-done.5
  44.0 0.0 copy-start.3
  44.0 1.6 %pad_maximum_fusion = bf16[4,2048,128]{2,1,0:T(8,128)(2,1)S(1)} fusion(bf16[1,2048,128]{2,1,0:T(8,128)(2,1)S(1)} %bitcast.49, bf16[1,2048,128]{2,1,0:T(8,128)(2,1)} %bitcast.50, bf16[1,2048,128]{2,1,0:T(8,128)(2,1)} %bitcast.51, bf16[1,2048,128]{2,1,0:T(8,128)(2,1)S(1)} %bitcast.47), kind=kLoop, calls=%fused_computation.10 | loop fusion | flops 3145728 | bytes 4194304 | tf_op jit(solution)/shard_map/stack | solution.py:282
  45.7 0.6 copy.44
  46.3 0.3 copy-done.3
  46.5 5.0 %shard_map.83 = bf16[4096,128]{1,0:T(8,128)(2,1)} custom-call(s32[4096]{0:T(1024)} %bitcast.60, bf16[16384,128]{1,0:T(8,128)(2,1)S(1)} %copy-done.3), custom_call_target="tpu_custom_call" | custom-call | tf_op jit(solution)/shard_map/pallas_call | solution.py:43
  51.6 0.0 copy-start.2
  51.6 3.7 %all-to-all-start.2 = ((bf16[8,512,128]{2,1,0:T(8,128)(2,1)}), bf16[8,512,128]{2,1,0:T(8,128)(2,1)S(1)}, u32[]{:S(2)}, u32[]{:S(2)}) async-start(bf16[8,512,128]{2,1,0:T(8,128)(2,1)} %bitcast.43), calls=%async_computation.2 | async-start | bytes 2097152 | tf_op jit(solution)/shard_map/all_to_all | solution.py:300
  55.3 0.1 reshape_squeeze.9
  55.4 0.0 copy-done.2
  55.4 0.8 gather_fusion.3
  56.2 0.6 slice_reduce_fusion
  57.5 24.1 %all-to-all-done.2 = bf16[8,512,128]{2,1,0:T(8,128)(2,1)S(1)} async-done(((bf16[8,512,128]{2,1,0:T(8,128)(2,1)}), bf16[8,512,128]{2,1,0:T(8,128)(2,1)S(1)}, u32[]{:S(2)}, u32[]{:S(2)}) %all-to-all-start.2) | async-done | bytes 1048608 | tf_op jit(solution)/shard_map/all_to_all | solution.py:300
  81.6 0.0 copy-start.6
  81.6 20.0 %conditional.1 = (f32[64,256]{1,0:T(8,128)S(1)}) conditional(s32[]{:T(128)} %convert_element_type.10, (s32[32,256]{1,0:T(8,128)S(1)}, bf16[8,512,128]{2,1,0:T(8,128)(2,1)S(1)}, s32[64]{0:T(128)S(1)}, s32[64]{0:T(128)S(1)}, f32[64]{0:T(128)S(1)}, /*index=5*/s32[4]{0:T(128)S(1)}, bf16[256,128,128]{2,1,0:T(8,128)(2,1)}, ...), branch_computations={%region_2.3_spmd, %region_3.4_spmd} | conditional | flops 1138688 | bytes 147079264 | solution.py:320
  81.6 0.6 copy.41
  82.2 19.4 %branch_0_fun.1 = f32[64,256]{1,0:T(8,128)S(1)} custom-call(s32[64]{0:T(128)S(1)} %get-tuple-element.43.chosen, s32[8192]{0:T(1024)} %bitcast.52, s32[64]{0:T(128)S(1)} %get-tuple-element.45.lengths, f32[64]{0:T(128)S(1)} %get-tuple-element.46.scales, s32[4]{0:T(128)S(1)} %get-tuple-element.47.holder, bf16[4096,128]{1,0:T(8,128)(2,1)S(1)} %bitcast.42, ...), custom_call_target="tpu_custom_call" | custom-call | tf_op jit(solution)/shard_map/cond/branch_0_fun/pallas_call | solution.py:112
  101.7 0.0 copy-start.1
  101.7 0.1 reshape.134
  101.8 0.1 reduce_sum.22
  101.9 0.1 reshape.169
  102.0 9.9 %all_to_all.33 = f32[32,1,128]{2,1,0:T(1,128)S(1)} all-to-all(f32[32,1,128]{2,1,0:T(1,128)S(1)} %reshape.169), channel_id=1, replica_groups=mesh['group'=4,'member'=8] {'group','member'}, dimensions={0} | all-to-all | bytes 32768 | tf_op jit(solution)/shard_map/all_to_all | solution.py:322
  111.9 0.5 broadcast.104
  112.4 0.7 reduce
  113.1 0.1 reshape.170
  113.2 0.1 copy.39
  113.3 0.0 copy-done.6
  113.3 1.3 %select_reduce_fusion = f32[64,128]{1,0:T(8,128)} fusion(f32[64,64]{1,0:T(8,128)S(1)} %copy.39, s32[64,128]{1,0:T(8,128)S(1)} %copy-done.6), kind=kLoop, calls=%fused_computation.11 | loop fusion | flops 1564672 | bytes 81920 | tf_op jit(solution)/shard_map/reduce_sum | solution.py:325
  114.6 0.0 copy-done.1
  (11 shorter events, 0.1 us)
Async XLA Ops:
  0.0 5.4 %copy-start = (s32[256,128]{1,0:T(8,128)S(1)}, s32[256,128]{1,0:T(8,128)}, u32[]{:S(2)}) copy-start(s32[256,128]{1,0:T(8,128)} %param.13) | copy-start | bytes 393220
  1.3 41.8 %collective-permute-start.2 = (bf16[2048,128]{1,0:T(8,128)(2,1)S(1)}, bf16[2048,128]{1,0:T(8,128)(2,1)S(1)}, u32[]{:S(2)}, u32[]{:S(2)}) collective-permute-start(bf16[2048,128]{1,0:T(8,128)(2,1)S(1)} %bitcast.44), channel_id=1, source_target_pairs={{0,24},{8,0},{16,8},{24,16},{1,25},{9,1},{17,9},{25,17},{2,26},{10... | collective-permute-start | bytes 1572872 | tf_op jit(solution)/shard_map/ppermute | solution.py:268
  3.7 39.3 %collective-permute-start.1 = (bf16[2048,128]{1,0:T(8,128)(2,1)S(1)}, bf16[2048,128]{1,0:T(8,128)(2,1)S(1)}, u32[]{:S(2)}, u32[]{:S(2)}) collective-permute-start(bf16[2048,128]{1,0:T(8,128)(2,1)S(1)} %bitcast.45), channel_id=1, source_target_pairs={{0,16},{8,24},{16,0},{24,8},{1,17},{9,25},{17,1},{25,9},{2,18},{10... | collective-permute-start | bytes 1572872 | tf_op jit(solution)/shard_map/ppermute | solution.py:268
  4.4 38.7 %collective-permute-start = (bf16[2048,128]{1,0:T(8,128)(2,1)S(1)}, bf16[2048,128]{1,0:T(8,128)(2,1)S(1)}, u32[]{:S(2)}, u32[]{:S(2)}) collective-permute-start(bf16[2048,128]{1,0:T(8,128)(2,1)S(1)} %bitcast.46), channel_id=1, source_target_pairs={{0,8},{8,16},{16,24},{24,0},{1,9},{9,17},{17,25},{25,1},{2,10},{10... | collective-permute-start | bytes 1572872 | tf_op jit(solution)/shard_map/ppermute | solution.py:268
  43.1 0.8 copy-start.4
  43.1 1.0 copy-start.5
  44.0 2.5 %copy-start.3 = (bf16[16384,128]{1,0:T(8,128)(2,1)S(1)}, bf16[16384,128]{1,0:T(8,128)(2,1)}, u32[]{:S(2)}) copy-start(bf16[16384,128]{1,0:T(8,128)(2,1)} %table.1) | copy-start | bytes 12582916
  51.6 3.8 %copy-start.2 = (bf16[256]{0:T(256)(128)(2,1)S(1)}, bf16[256]{0:T(256)(128)(2,1)}, u32[]{:S(2)}) copy-start(bf16[256]{0:T(256)(128)(2,1)} %param.14) | copy-start | bytes 1540
  51.6 30.0 %all-to-all-start.2 = ((bf16[8,512,128]{2,1,0:T(8,128)(2,1)}), bf16[8,512,128]{2,1,0:T(8,128)(2,1)S(1)}, u32[]{:S(2)}, u32[]{:S(2)}) async-start(bf16[8,512,128]{2,1,0:T(8,128)(2,1)} %bitcast.43), calls=%async_computation.2 | async-start | bytes 2097152 | tf_op jit(solution)/shard_map/all_to_all | solution.py:300
  81.6 31.7 %copy-start.6 = (s32[64,128]{1,0:T(8,128)S(1)}, s32[64,128]{1,0:T(8,128)}, u32[]{:S(2)}) copy-start(s32[64,128]{1,0:T(8,128)} %param.17) | copy-start | bytes 98308
  101.7 12.9 %copy-start.1 = (s32[256,128]{1,0:T(8,128)S(1)}, s32[256,128]{1,0:T(8,128)}, u32[]{:S(2)}) copy-start(s32[256,128]{1,0:T(8,128)} %param.13) | copy-start | bytes 393220

commit v2 on v1

--- a/solution.py
+++ b/solution.py
@@ -139,14 +139,75 @@
     return out.reshape(slots, chunk // qcount, qcount).sum(axis=1)
 
 
-def pack_kernel(members, capacity, codes, place, lists, highest, seen, whole, ranks, sums):
+def exchange_kernel(axes, sizes, given, taken, send_sem, recv_sem):
+    count = given.shape[0]
+    me = jnp.int32(0)
+    for axis, size in zip(axes, sizes):
+        me = me * size + lax.axis_index(axis)
+
+    def device(peer):
+        where = {}
+        for axis, size in reversed(list(zip(axes, sizes))):
+            where[axis] = lax.rem(peer, size)
+            peer = peer // size
+        return where
+
+    def at_distance(d):
+        return lax.rem(me + d, count)
+
+    barrier = pltpu.get_barrier_semaphore()
+    for d in range(1, count):
+        pl.semaphore_signal(
+            barrier,
+            inc=1,
+            device_id=device(at_distance(d)),
+            device_id_type=pl.DeviceIdType.MESH,
+        )
+    taken[me] = given[me]
+    pl.semaphore_wait(barrier, count - 1)
+    copies = []
+    for d in range(1, count):
+        peer = at_distance(d)
+        copy = pltpu.make_async_remote_copy(
+            src_ref=given.at[peer],
+            dst_ref=taken.at[me],
+            send_sem=send_sem.at[d],
+            recv_sem=recv_sem.at[d],
+            device_id=device(peer),
+            device_id_type=pl.DeviceIdType.MESH,
+        )
+        copy.start()
+        copies.append(copy)
+    for copy in copies:
+        copy.wait()
+
+
+def exchange(given, axes, collective_id):
+    sizes = tuple(lax.axis_size(axis) for axis in axes)
+    count = given.shape[0]
+    return pl.pallas_call(
+        functools.partial(exchange_kernel, axes, sizes),
+        out_shape=jax.ShapeDtypeStruct(given.shape, given.dtype),
+        in_specs=[pl.BlockSpec(memory_space=pltpu.VMEM)],
+        out_specs=pl.BlockSpec(memory_space=pltpu.VMEM),
+        scratch_shapes=[
+            pltpu.SemaphoreType.DMA((count,)),
+            pltpu.SemaphoreType.DMA((count,)),
+        ],
+        compiler_params=pltpu.CompilerParams(
+            collective_id=collective_id, has_side_effects=True
+        ),
+    )(given)
+
+
+def pack_kernel(members, capacity, codes, place, lists, seen, whole, ranks, sums):
     steps, span = codes.shape
     lines = seen.shape[0]
     part = lines // members
     shard = part * GRAIN
     stripe = min(256, lines)
     bits = GRAIN.bit_length() - 1
-    list_lines = lists.shape[0]
+    list_lines = members * capacity // LANES
 
     def same(count, row, first=0):
         row = jnp.broadcast_to((row - first).astype(jnp.float32), (16, span))
@@ -196,7 +257,7 @@
         coarse = jnp.floor(rank * (1.0 / LANES))
         fine = rank - coarse * LANES
         whole[at, :] = jnp.concatenate([coarse, fine], axis=1)
-    highest[...] = jnp.broadcast_to(top, highest.shape)
+    top = jnp.max(top, axis=1, keepdims=True).astype(jnp.int32)
     ranks[...] = whole[...].T.astype(jnp.bfloat16)
 
     @pl.loop(0, steps, unroll=4)
@@ -232,7 +293,11 @@
     times = jnp.maximum(sums[2 * list_lines :, :], 1.0)
     low = (sums[:list_lines, :] / times + 0.5).astype(jnp.int32)
     high = (sums[list_lines : 2 * list_lines, :] / times + 0.5).astype(jnp.int32)
-    lists[...] = low + 256 * high
+    packed = low + 256 * high
+    own = capacity // LANES
+    for o in range(members):
+        lists[o, 0:own, :] = packed[o * own : (o + 1) * own, :]
+        lists[o, own:, :] = jnp.broadcast_to(top, (lists.shape[1] - own, LANES))
 
 
 def make_lists(wanted, members, shard, capacity):
@@ -240,12 +305,12 @@
     steps = wanted.size // span
     lines = members * shard // GRAIN
     list_lines = members * capacity // LANES
-    place, lists, highest = pl.pallas_call(
+    deep = (capacity // LANES // 8 + 1) * 8
+    place, lists = pl.pallas_call(
         functools.partial(pack_kernel, members, capacity),
         out_shape=(
             jax.ShapeDtypeStruct((steps, span), jnp.int32),
-            jax.ShapeDtypeStruct((list_lines, LANES), jnp.int32),
-            jax.ShapeDtypeStruct((8, GRAIN), jnp.float32),
+            jax.ShapeDtypeStruct((members, deep, LANES), jnp.int32),
         ),
         scratch_shapes=[
             pltpu.VMEM((lines, GRAIN), jnp.float32),
@@ -258,8 +323,7 @@
         ),
         compiler_params=pltpu.CompilerParams(vmem_limit_bytes=VMEM_LIMIT),
     )(wanted.reshape(steps, span))
-    overflow = jnp.max(highest) > capacity
-    return lists.reshape(members, capacity), place.reshape(-1), overflow
+    return lists, place.reshape(-1)
 
 
 def around(array, axis):
@@ -289,14 +353,12 @@
 
     lookups = slots * block
     capacity = -(-lookups // (2 * members * LANES)) * LANES
-    lists, place, overflow = make_lists(jnp.where(valid, codes, -1), members, shard, capacity)
-    flag = jnp.broadcast_to(overflow.astype(jnp.int32), (members, LANES))
-    asked = lax.all_to_all(
-        jnp.concatenate([lists, flag], axis=1), "member", split_axis=0, concat_axis=0, tiled=True
-    )
+    lists, place = make_lists(jnp.where(valid, codes, -1), members, shard, capacity)
+    asked = exchange(lists, ("member",), 0)
     asked, every_query = lax.optimization_barrier((asked, every_query))
-    overflow = jnp.max(asked[:, capacity:]) > 0
-    rows = fetch_rows(asked[:, :capacity].reshape(-1), centroids)
+    own = capacity // LANES
+    overflow = jnp.max(asked[:, own]) > capacity
+    rows = fetch_rows(asked[:, :own].reshape(-1), centroids)
     received = lax.all_to_all(rows, "member", split_axis=0, concat_axis=0, tiled=True)
 
     me = lax.axis_index("group")

time: 116 us -> 112 us (0.966)
  blocking collectives: 22.2 us -> 10.7 us
  Pallas kernels: 43 us -> 51.9 us
  starting transfers between devices: 6.95 us -> 8.97 us
  waiting for transfers between devices: 24.1 us -> 22.8 us
    all_to_all x1 -> x0, blocking collectives: 12.3 us -> none  [body(): lax.all_to_all(jnp.concatenate([lists, flag], axis=1), 'member', split_ax...]
    pallas_call x0 -> x1, Pallas kernels: none -> 8.37 us  [exchange(): pl.pallas_call(functools.partial(exchange_kernel, axes, sizes), out_shape...]
    all_to_all x1, starting transfers between devices: 3.69 us -> 5.71 us  [body(): lax.all_to_all(rows, 'member', split_axis=0, concat_axis=0, tiled=True)]
    slice x0 -> x1, local copies, waits for them, and re-layouts: none -> 1.37 us  [body(): rows = fetch_rows(asked[:, :own].reshape(-1), centroids)]
    all_to_all x1, waiting for transfers between devices: 24.1 us -> 22.8 us  [body(): lax.all_to_all(rows, 'member', split_axis=0, concat_axis=0, tiled=True)]
    unnamed x20 -> x17, local copies, waits for them, and re-layouts: 2.79 us -> 1.9 us
  transfers between devices with their start and end apart: 4 -> 4, of which waited for: 1 -> 1; matrix products, arithmetic and copies ran while one was open for 7% -> 6% of each run, Pallas kernels for 16% -> 24%
where the time goes in v2:
time: 112 us; the launch traced here: 111 us
  Pallas kernels  51.9 us (46%)
  waiting for transfers between devices  22.8 us (20%)
  blocking collectives  10.7 us (10%)
  local copies, waits for them, and re-layouts  9.5 us (8%)
  starting transfers between devices  8.97 us (8%)
  other arithmetic  6.46 us (6%)
    all_to_all x1, waiting for transfers between devices, body(): lax.all_to_all(rows, 'member', split_axis=0, concat_axis=0, tiled=True)  22.8 us
    pallas_call x1, Pallas kernels, score(): pl.pallas_call(functools.partial(score_kernel, docs, columns // qcount),...  19.4 us
    pallas_call x1, Pallas kernels, make_lists(): pl.pallas_call(functools.partial(pack_kernel, members, capacity), out_sha...  18.7 us
    all_to_all x1, blocking collectives, body(): lax.all_to_all(local, ('group', 'member'), split_axis=0, concat_axis=0, t...  10.7 us
    pallas_call x1, Pallas kernels, exchange(): pl.pallas_call(functools.partial(exchange_kernel, axes, sizes), out_shape...  8.37 us
    all_to_all x1, starting transfers between devices, body(): lax.all_to_all(rows, 'member', split_axis=0, concat_axis=0, tiled=True)  5.71 us
    pallas_call x1, Pallas kernels, fetch_rows(): pl.pallas_call(fetch_kernel, out_shape=jax.ShapeDtypeStruct((count, width...  5.44 us
    ppermute x3, starting transfers between devices, around(): lax.ppermute(array, axis, [(i, (i + d) % size) for i in range(size)])  3.26 us
  transfers between devices with their start and end apart: 4, of which 1 were waited for; matrix products, arithmetic and copies ran while one was open for 6% of the time, Pallas kernels for 24%

profile of v2, /device:TPU:0, one launch (start us, length us, event | category | flops | bytes accessed | tf_op | source)
XLA Modules:
  0.0 111.2 jit_solution(3038538440826959564)
XLA Ops:
  0.0 0.0 copy-start
  0.0 1.3 %copy.28 = bf16[32,64,128]{2,1,0:T(8,128)(2,1)S(1)} copy(bf16[32,64,128]{2,0,1:T(8,128)(2,1)} %bitcast.43) | data formatting | bytes 1048576 | tf_op jit(solution)/shard_map/transpose | solution.py:345
  1.3 2.5 %collective-permute-start.2 = (bf16[2048,128]{1,0:T(8,128)(2,1)S(1)}, bf16[2048,128]{1,0:T(8,128)(2,1)S(1)}, u32[]{:S(2)}, u32[]{:S(2)}) collective-permute-start(bf16[2048,128]{1,0:T(8,128)(2,1)S(1)} %bitcast.39), channel_id=1, source_target_pairs={{0,24},{8,0},{16,8},{24,16},{1,25},{9,1},{17,9},{25,17},{2,26},{10... | collective-permute-start | bytes 1572872 | tf_op jit(solution)/shard_map/ppermute | solution.py:332
  3.7 0.6 collective-permute-start.1
  4.4 0.2 collective-permute-start
  4.6 0.8 copy.24
  5.3 0.1 reshape_squeeze.8
  5.4 0.0 copy-done
  5.5 0.6 gather_fusion.2
  6.1 1.5 %gather_fusion.1 = s32[64]{0:T(128)S(1)} fusion(s32[256]{0:T(256)} %param.15, s32[1024]{0:T(1024)S(1)} %pad_clamp_fusion), kind=kCustom, calls=%fused_computation.1 | custom fusion | bytes 768 | tf_op jit(solution)/shard_map/jit(_take)/gather | solution.py:351
  7.5 0.1 gather.21
  7.6 0.1 copy.25
  7.7 0.7 broadcast_select_fusion.2
  8.4 0.1 copy.26
  8.5 0.1 copy.27
  8.6 0.1 lt.85
  8.7 0.1 broadcast_in_dim.68
  8.8 0.6 select_select_fusion.codes
  9.4 18.7 %shard_map.82 = (s32[32,256]{1,0:T(8,128)S(1)}, s32[8,8,128]{2,1,0:T(8,128)}) custom-call(s32[32,256]{1,0:T(8,128)} %select_select_fusion.codes), custom_call_target="tpu_custom_call" | custom-call | flops 25769803776 | bytes 98304 | tf_op jit(solution)/shard_map/pallas_call | solution.py:309
  28.1 8.4 %shard_map.83 = s32[8,8,128]{2,1,0:T(8,128)} custom-call(s32[8,8,128]{2,1,0:T(8,128)} %get-tuple-element.63.given), custom_call_target="tpu_custom_call" | custom-call | tf_op jit(solution)/shard_map/pallas_call | solution.py:188
  36.5 0.0 collective-permute-done.2
  36.5 0.0 collective-permute-done.1
  36.5 0.0 copy-start.4
  36.5 0.0 collective-permute-done
  36.6 0.0 copy-start.5
  36.6 0.8 copy-done.4
  37.3 0.2 copy-done.5
  37.5 0.0 copy-start.3
  37.5 1.6 %pad_maximum_fusion = bf16[4,2048,128]{2,1,0:T(8,128)(2,1)S(1)} fusion(bf16[1,2048,128]{2,1,0:T(8,128)(2,1)S(1)} %bitcast.44, bf16[1,2048,128]{2,1,0:T(8,128)(2,1)} %bitcast.45, bf16[1,2048,128]{2,1,0:T(8,128)(2,1)} %bitcast.46, bf16[1,2048,128]{2,1,0:T(8,128)(2,1)S(1)} %bitcast.42), kind=kLoop, calls=%fused_computation.10 | loop fusion | flops 3145728 | bytes 4194304 | tf_op jit(solution)/shard_map/stack | solution.py:346
  39.1 1.4 %slice.7 = s32[8,4,128]{2,1,0:T(4,128)} slice(s32[8,8,128]{2,1,0:T(8,128)} %shard_map.83), slice={[0:8], [0:4], [0:128]} | slice | bytes 32768 | tf_op jit(solution)/shard_map/slice | solution.py:361
  40.5 0.0 copy-done.3
  40.5 5.4 %shard_map.84 = bf16[4096,128]{1,0:T(8,128)(2,1)} custom-call(s32[4096]{0:T(1024)} %bitcast.53, bf16[16384,128]{1,0:T(8,128)(2,1)S(1)} %copy-done.3), custom_call_target="tpu_custom_call" | custom-call | tf_op jit(solution)/shard_map/pallas_call | solution.py:43
  45.9 0.0 copy-start.2
  45.9 5.7 %all-to-all-start.1 = ((bf16[8,512,128]{2,1,0:T(8,128)(2,1)}), bf16[8,512,128]{2,1,0:T(8,128)(2,1)S(1)}, u32[]{:S(2)}, u32[]{:S(2)}) async-start(bf16[8,512,128]{2,1,0:T(8,128)(2,1)} %bitcast.38), calls=%async_computation.1 | async-start | bytes 2097152 | tf_op jit(solution)/shard_map/all_to_all | solution.py:362
  51.6 0.1 reshape_squeeze.9
  51.7 0.0 copy-done.2
  51.7 0.8 gather_fusion.3
  52.6 1.4 %slice_reduce_fusion = s32[]{:T(128)} fusion(s32[8,8,128]{2,1,0:T(8,128)} %shard_map.83), kind=kLoop, calls=%fused_computation.16 | loop fusion | flops 1023 | bytes 4100 | tf_op jit(solution)/shard_map/reduce_max | solution.py:360
  54.6 22.8 %all-to-all-done.1 = bf16[8,512,128]{2,1,0:T(8,128)(2,1)S(1)} async-done(((bf16[8,512,128]{2,1,0:T(8,128)(2,1)}), bf16[8,512,128]{2,1,0:T(8,128)(2,1)S(1)}, u32[]{:S(2)}, u32[]{:S(2)}) %all-to-all-start.1) | async-done | bytes 1048608 | tf_op jit(solution)/shard_map/all_to_all | solution.py:362
  77.4 0.0 copy-start.6
  77.4 20.1 %conditional.1 = (f32[64,256]{1,0:T(8,128)S(1)}) conditional(s32[]{:T(128)} %convert_element_type.6, (s32[32,256]{1,0:T(8,128)S(1)}, bf16[8,512,128]{2,1,0:T(8,128)(2,1)S(1)}, s32[64]{0:T(128)S(1)}, s32[64]{0:T(128)S(1)}, f32[64]{0:T(128)S(1)}, /*index=5*/s32[4]{0:T(128)S(1)}, bf16[256,128,128]{2,1,0:T(8,128)(2,1)}, ...), branch_computations={%region_1.2_spmd, %region_2.3_spmd} | conditional | flops 1138688 | bytes 147079264 | solution.py:382
  77.4 0.6 copy.32
  78.1 19.4 %branch_0_fun.1 = f32[64,256]{1,0:T(8,128)S(1)} custom-call(s32[64]{0:T(128)S(1)} %get-tuple-element.43.chosen, s32[8192]{0:T(1024)} %bitcast.47, s32[64]{0:T(128)S(1)} %get-tuple-element.45.lengths, f32[64]{0:T(128)S(1)} %get-tuple-element.46.scales, s32[4]{0:T(128)S(1)} %get-tuple-element.47.holder, bf16[4096,128]{1,0:T(8,128)(2,1)S(1)} %bitcast.37, ...), custom_call_target="tpu_custom_call" | custom-call | tf_op jit(solution)/shard_map/cond/branch_0_fun/pallas_call | solution.py:112
  97.5 0.0 copy-start.1
  97.5 0.1 reshape.128
  97.6 0.1 reduce_sum.22
  97.7 0.1 reshape.163
  97.8 10.7 %all_to_all.20 = f32[32,1,128]{2,1,0:T(1,128)S(1)} all-to-all(f32[32,1,128]{2,1,0:T(1,128)S(1)} %reshape.163), channel_id=1, replica_groups=mesh['group'=4,'member'=8] {'group','member'}, dimensions={0} | all-to-all | bytes 32768 | tf_op jit(solution)/shard_map/all_to_all | solution.py:384
  108.5 0.5 broadcast.102
  109.0 0.7 reduce.1
  109.7 0.1 reshape.164
  109.8 0.1 copy.31
  109.9 0.0 copy-done.6
  109.9 1.3 %select_reduce_fusion = f32[64,128]{1,0:T(8,128)} fusion(f32[64,64]{1,0:T(8,128)S(1)} %copy.31, s32[64,128]{1,0:T(8,128)S(1)} %copy-done.6), kind=kLoop, calls=%fused_computation.11 | loop fusion | flops 1564672 | bytes 81920 | tf_op jit(solution)/shard_map/reduce_sum | solution.py:387
  111.2 0.0 copy-done.1
  (7 shorter events, 0.0 us)
Async XLA Ops:
  0.0 5.4 %copy-start = (s32[256,128]{1,0:T(8,128)S(1)}, s32[256,128]{1,0:T(8,128)}, u32[]{:S(2)}) copy-start(s32[256,128]{1,0:T(8,128)} %param.13) | copy-start | bytes 393220
  1.3 35.2 %collective-permute-start.2 = (bf16[2048,128]{1,0:T(8,128)(2,1)S(1)}, bf16[2048,128]{1,0:T(8,128)(2,1)S(1)}, u32[]{:S(2)}, u32[]{:S(2)}) collective-permute-start(bf16[2048,128]{1,0:T(8,128)(2,1)S(1)} %bitcast.39), channel_id=1, source_target_pairs={{0,24},{8,0},{16,8},{24,16},{1,25},{9,1},{17,9},{25,17},{2,26},{10... | collective-permute-start | bytes 1572872 | tf_op jit(solution)/shard_map/ppermute | solution.py:332
  3.7 32.8 %collective-permute-start.1 = (bf16[2048,128]{1,0:T(8,128)(2,1)S(1)}, bf16[2048,128]{1,0:T(8,128)(2,1)S(1)}, u32[]{:S(2)}, u32[]{:S(2)}) collective-permute-start(bf16[2048,128]{1,0:T(8,128)(2,1)S(1)} %bitcast.40), channel_id=1, source_target_pairs={{0,16},{8,24},{16,0},{24,8},{1,17},{9,25},{17,1},{25,9},{2,18},{10... | collective-permute-start | bytes 1572872 | tf_op jit(solution)/shard_map/ppermute | solution.py:332
  4.4 32.2 %collective-permute-start = (bf16[2048,128]{1,0:T(8,128)(2,1)S(1)}, bf16[2048,128]{1,0:T(8,128)(2,1)S(1)}, u32[]{:S(2)}, u32[]{:S(2)}) collective-permute-start(bf16[2048,128]{1,0:T(8,128)(2,1)S(1)} %bitcast.41), channel_id=1, source_target_pairs={{0,8},{8,16},{16,24},{24,0},{1,9},{9,17},{17,25},{25,1},{2,10},{10... | collective-permute-start | bytes 1572872 | tf_op jit(solution)/shard_map/ppermute | solution.py:332
  36.5 0.8 copy-start.4
  36.6 0.9 copy-start.5
  37.5 3.0 %copy-start.3 = (bf16[16384,128]{1,0:T(8,128)(2,1)S(1)}, bf16[16384,128]{1,0:T(8,128)(2,1)}, u32[]{:S(2)}) copy-start(bf16[16384,128]{1,0:T(8,128)(2,1)} %table.1) | copy-start | bytes 12582916
  45.9 5.8 %copy-start.2 = (bf16[256]{0:T(256)(128)(2,1)S(1)}, bf16[256]{0:T(256)(128)(2,1)}, u32[]{:S(2)}) copy-start(bf16[256]{0:T(256)(128)(2,1)} %param.14) | copy-start | bytes 1540
  45.9 31.5 %all-to-all-start.1 = ((bf16[8,512,128]{2,1,0:T(8,128)(2,1)}), bf16[8,512,128]{2,1,0:T(8,128)(2,1)S(1)}, u32[]{:S(2)}, u32[]{:S(2)}) async-start(bf16[8,512,128]{2,1,0:T(8,128)(2,1)} %bitcast.38), calls=%async_computation.1 | async-start | bytes 2097152 | tf_op jit(solution)/shard_map/all_to_all | solution.py:362
  77.4 32.5 %copy-start.6 = (s32[64,128]{1,0:T(8,128)S(1)}, s32[64,128]{1,0:T(8,128)}, u32[]{:S(2)}) copy-start(s32[64,128]{1,0:T(8,128)} %param.17) | copy-start | bytes 98308
  97.5 13.7 %copy-start.1 = (s32[256,128]{1,0:T(8,128)S(1)}, s32[256,128]{1,0:T(8,128)}, u32[]{:S(2)}) copy-start(s32[256,128]{1,0:T(8,128)} %param.13) | copy-start | bytes 393220

commit v3 on v2

--- a/solution.py
+++ b/solution.py
@@ -207,7 +207,7 @@
     shard = part * GRAIN
     stripe = min(256, lines)
     bits = GRAIN.bit_length() - 1
-    list_lines = members * capacity // LANES
+    list_lines = -(-members * capacity // LANES // 16) * 16
 
     def same(count, row, first=0):
         row = jnp.broadcast_to((row - first).astype(jnp.float32), (16, span))
@@ -304,7 +304,7 @@
     span = 256
     steps = wanted.size // span
     lines = members * shard // GRAIN
-    list_lines = members * capacity // LANES
+    list_lines = -(-members * capacity // LANES // 16) * 16
     deep = (capacity // LANES // 8 + 1) * 8
     place, lists = pl.pallas_call(
         functools.partial(pack_kernel, members, capacity),
@@ -352,7 +352,7 @@
     valid = jnp.arange(block, dtype=jnp.int32)[None, :] < lengths[:, None]
 
     lookups = slots * block
-    capacity = -(-lookups // (2 * members * LANES)) * LANES
+    capacity = -(-3 * lookups // (8 * members * LANES)) * LANES
     lists, place = make_lists(jnp.where(valid, codes, -1), members, shard, capacity)
     asked = exchange(lists, ("member",), 0)
     asked, every_query = lax.optimization_barrier((asked, every_query))
@@ -380,8 +380,8 @@
         )
 
     local = lax.cond(overflow, whole_table, listed)
-    local = local.reshape(groups * members, capacity_sent, qcount)
-    returned = lax.all_to_all(local, ("group", "member"), split_axis=0, concat_axis=0, tiled=True)
+    local = local.reshape(groups * members, 1, capacity_sent * qcount)
+    returned = exchange(local, ("group", "member"), 1)
     dense = returned.reshape(-1, qcount).T
     hit = cand[:, :, None] == jnp.arange(dense.shape[1], dtype=jnp.int32)
     return jnp.sum(jnp.where(hit, dense[:, None, :], 0.0), axis=2)

time: 112 us -> 108 us (0.964)
  Pallas kernels: 51.9 us -> 63.1 us
  blocking collectives: 10.7 us -> 0 us
  waiting for transfers between devices: 22.8 us -> 18.4 us
    all_to_all x1 -> x0, blocking collectives: 10.7 us -> none  [body(): lax.all_to_all(local, ('group', 'member'), split_axis=0, concat_axis=0, t...]
    pallas_call x1 -> x2, Pallas kernels: 8.37 us -> 17.6 us  [exchange(): pl.pallas_call(functools.partial(exchange_kernel, axes, sizes), out_shape...]
    all_to_all x1, waiting for transfers between devices: 22.8 us -> 18.4 us  [body(): lax.all_to_all(rows, 'member', split_axis=0, concat_axis=0, tiled=True)]
    pallas_call x1, Pallas kernels: 5.44 us -> 7.06 us  [fetch_rows(): pl.pallas_call(fetch_kernel, out_shape=jax.ShapeDtypeStruct((count, width...]
    pallas_call x0 -> x1, other arithmetic: none -> 1.4 us  [exchange(): pl.pallas_call(functools.partial(exchange_kernel, axes, sizes), out_shape...]
    reshape x0 -> x3, local copies, waits for them, and re-layouts: none -> 1.37 us  [the longest x1 0.69 us: body(): local = local.reshape(groups * members, 1, capacity_sent * qcount)]
    slice x1 -> x2, local copies, waits for them, and re-layouts: 1.37 us -> 0.01 us  [body(): rows = fetch_rows(asked[:, :own].reshape(-1), centroids)]
  transfers between devices with their start and end apart: 4 -> 4, of which waited for: 1 -> 1; matrix products, arithmetic and copies ran while one was open for 6% -> 6% of each run, Pallas kernels for 24% -> 25%
where the time goes in v3:
time: 108 us; the launch traced here: 107 us
  Pallas kernels  63.1 us (58%)
  waiting for transfers between devices  18.4 us (17%)
  local copies, waits for them, and re-layouts  9.34 us (9%)
  starting transfers between devices  8.98 us (8%)
  other arithmetic  6.28 us (6%)
    pallas_call x1, Pallas kernels, score(): pl.pallas_call(functools.partial(score_kernel, docs, columns // qcount),...  19.8 us
    pallas_call x1, Pallas kernels, make_lists(): pl.pallas_call(functools.partial(pack_kernel, members, capacity), out_sha...  18.7 us
    all_to_all x1, waiting for transfers between devices, body(): lax.all_to_all(rows, 'member', split_axis=0, concat_axis=0, tiled=True)  18.4 us
    pallas_call x2, Pallas kernels, exchange(): pl.pallas_call(functools.partial(exchange_kernel, axes, sizes), out_shape...  17.6 us
    pallas_call x1, Pallas kernels, fetch_rows(): pl.pallas_call(fetch_kernel, out_shape=jax.ShapeDtypeStruct((count, width...  7.06 us
    all_to_all x1, starting transfers between devices, body(): lax.all_to_all(rows, 'member', split_axis=0, concat_axis=0, tiled=True)  5.71 us
    ppermute x3, starting transfers between devices, around(): lax.ppermute(array, axis, [(i, (i + d) % size) for i in range(size)])  3.26 us
  transfers between devices with their start and end apart: 4, of which 1 were waited for; matrix products, arithmetic and copies ran while one was open for 6% of the time, Pallas kernels for 25%

profile of v3, /device:TPU:0, one launch (start us, length us, event | category | flops | bytes accessed | tf_op | source)
XLA Modules:
  0.0 107.0 jit_solution(6427306030594060931)
XLA Ops:
  0.0 0.0 copy-start
  0.0 1.3 %copy.29 = bf16[32,64,128]{2,1,0:T(8,128)(2,1)S(1)} copy(bf16[32,64,128]{2,0,1:T(8,128)(2,1)} %bitcast.39) | data formatting | bytes 1048576 | tf_op jit(solution)/shard_map/transpose | solution.py:345
  1.3 2.5 %collective-permute-start.2 = (bf16[2048,128]{1,0:T(8,128)(2,1)S(1)}, bf16[2048,128]{1,0:T(8,128)(2,1)S(1)}, u32[]{:S(2)}, u32[]{:S(2)}) collective-permute-start(bf16[2048,128]{1,0:T(8,128)(2,1)S(1)} %bitcast.35), channel_id=1, source_target_pairs={{0,24},{8,0},{16,8},{24,16},{1,25},{9,1},{17,9},{25,17},{2,26},{10... | collective-permute-start | bytes 1572872 | tf_op jit(solution)/shard_map/ppermute | solution.py:332
  3.7 0.6 collective-permute-start.1
  4.4 0.2 collective-permute-start
  4.6 0.8 copy.25
  5.3 0.1 reshape_squeeze.8
  5.4 0.0 copy-done
  5.5 0.6 gather_fusion.2
  6.1 1.5 %gather_fusion.1 = s32[64]{0:T(128)S(1)} fusion(s32[256]{0:T(256)} %param.15, s32[1024]{0:T(1024)S(1)} %pad_clamp_fusion), kind=kCustom, calls=%fused_computation.1 | custom fusion | bytes 768 | tf_op jit(solution)/shard_map/jit(_take)/gather | solution.py:351
  7.5 0.1 gather.21
  7.6 0.1 copy.26
  7.7 0.7 broadcast_select_fusion.2
  8.4 0.1 copy.27
  8.5 0.1 copy.28
  8.6 0.1 lt.85
  8.7 0.1 broadcast_in_dim.68
  8.8 0.6 select_select_fusion.codes
  9.4 18.7 %shard_map.82 = (s32[32,256]{1,0:T(8,128)S(1)}, s32[8,8,128]{2,1,0:T(8,128)}) custom-call(s32[32,256]{1,0:T(8,128)} %select_select_fusion.codes), custom_call_target="tpu_custom_call" | custom-call | flops 25769803776 | bytes 98304 | tf_op jit(solution)/shard_map/pallas_call | solution.py:309
  28.1 8.3 %shard_map.83 = s32[8,8,128]{2,1,0:T(8,128)} custom-call(s32[8,8,128]{2,1,0:T(8,128)} %get-tuple-element.63.given), custom_call_target="tpu_custom_call" | custom-call | tf_op jit(solution)/shard_map/pallas_call | solution.py:188
  36.5 0.0 collective-permute-done.2
  36.5 0.0 collective-permute-done.1
  36.5 0.0 copy-start.3
  36.5 0.0 collective-permute-done
  36.5 0.0 copy-start.4
  36.5 0.8 copy-done.3
  37.3 0.2 copy-done.4
  37.5 0.0 slice-start
  37.5 1.5 %pad_maximum_fusion = bf16[4,2048,128]{2,1,0:T(8,128)(2,1)S(1)} fusion(bf16[1,2048,128]{2,1,0:T(8,128)(2,1)S(1)} %bitcast.40, bf16[1,2048,128]{2,1,0:T(8,128)(2,1)} %bitcast.41, bf16[1,2048,128]{2,1,0:T(8,128)(2,1)} %bitcast.42, bf16[1,2048,128]{2,1,0:T(8,128)(2,1)S(1)} %bitcast.38), kind=kLoop, calls=%fused_computation.10 | loop fusion | flops 3145728 | bytes 4194304 | tf_op jit(solution)/shard_map/stack | solution.py:346
  38.9 0.0 slice-done
  38.9 0.6 reshape.127.entries
  39.6 0.0 copy-start.2
  39.6 7.1 %shard_map.84 = bf16[3072,128]{1,0:T(8,128)(2,1)} custom-call(s32[3072]{0:T(1024)} %reshape.127.entries, bf16[16384,128]{1,0:T(8,128)(2,1)} %table.1), custom_call_target="tpu_custom_call" | custom-call | tf_op jit(solution)/shard_map/pallas_call | solution.py:43
  46.6 0.0 copy-start.5
  46.6 5.7 %all-to-all-start.1 = ((bf16[8,384,128]{2,1,0:T(8,128)(2,1)}), bf16[8,384,128]{2,1,0:T(8,128)(2,1)S(1)}, u32[]{:S(2)}, u32[]{:S(2)}) async-start(bf16[8,384,128]{2,1,0:T(8,128)(2,1)} %bitcast.34), calls=%async_computation.1 | async-start | bytes 1572864 | tf_op jit(solution)/shard_map/all_to_all | solution.py:362
  52.3 0.1 reshape_squeeze.9
  52.4 0.0 copy-done.2
  52.5 0.8 gather_fusion.3
  53.3 0.0 copy-done.5
  53.3 0.6 slice_reduce_fusion
  54.6 18.4 %all-to-all-done.1 = bf16[8,384,128]{2,1,0:T(8,128)(2,1)S(1)} async-done(((bf16[8,384,128]{2,1,0:T(8,128)(2,1)}), bf16[8,384,128]{2,1,0:T(8,128)(2,1)S(1)}, u32[]{:S(2)}, u32[]{:S(2)}) %all-to-all-start.1) | async-done | bytes 786464 | tf_op jit(solution)/shard_map/all_to_all | solution.py:362
  73.0 0.0 copy-start.6
  73.0 20.4 %conditional.1 = (f32[64,256]{1,0:T(8,128)S(1)}) conditional(s32[]{:T(128)} %convert_element_type.6, (s32[32,256]{1,0:T(8,128)S(1)}, bf16[8,384,128]{2,1,0:T(8,128)(2,1)S(1)}, s32[64]{0:T(128)S(1)}, s32[64]{0:T(128)S(1)}, f32[64]{0:T(128)S(1)}, /*index=5*/s32[4]{0:T(128)S(1)}, bf16[256,128,128]{2,1,0:T(8,128)(2,1)}, ...), branch_computations={%region_1.2_spmd, %region_2.3_spmd} | conditional | flops 1138688 | bytes 147079264 | solution.py:382
  73.0 0.6 copy.33
  73.6 19.8 %branch_0_fun.1 = f32[64,256]{1,0:T(8,128)S(1)} custom-call(s32[64]{0:T(128)S(1)} %get-tuple-element.43.chosen, s32[8192]{0:T(1024)} %bitcast.43, s32[64]{0:T(128)S(1)} %get-tuple-element.45.lengths, f32[64]{0:T(128)S(1)} %get-tuple-element.46.scales, s32[4]{0:T(128)S(1)} %get-tuple-element.47.holder, bf16[3072,128]{1,0:T(8,128)(2,1)S(1)} %bitcast.33, ...), custom_call_target="tpu_custom_call" | custom-call | tf_op jit(solution)/shard_map/cond/branch_0_fun/pallas_call | solution.py:112
  93.4 0.0 copy-start.1
  93.4 0.1 reshape.128
  93.5 0.1 reduce_sum.22
  93.6 0.7 reshape.129.given
  94.3 9.2 %shard_map.85 = f32[32,1,128]{2,1,0:T(1,128)} custom-call(f32[32,1,128]{2,1,0:T(1,128)} %reshape.129.given), custom_call_target="tpu_custom_call" | custom-call | tf_op jit(solution)/shard_map/pallas_call | solution.py:188
  103.6 0.5 broadcast.105
  104.1 1.4 %reduce.4 = f32[32,128]{1,0:T(8,128)S(1)} reduce(f32[32,1,128]{2,1,0:T(1,128)} %shard_map.85, f32[]{:T(128)} %broadcast.105), dimensions={1}, to_apply=%pallas_call.25.reduce_sub_computation.3 | reduce | bytes 32772 | tf_op jit(solution)/shard_map/pallas_call | solution.py:188
  105.5 0.1 reshape.130
  105.6 0.1 copy.32
  105.6 0.0 copy-done.6
  105.6 1.3 %select_reduce_fusion = f32[64,128]{1,0:T(8,128)} fusion(f32[64,64]{1,0:T(8,128)S(1)} %copy.32, s32[64,128]{1,0:T(8,128)S(1)} %copy-done.6), kind=kLoop, calls=%fused_computation.11 | loop fusion | flops 1564672 | bytes 81920 | tf_op jit(solution)/shard_map/reduce_sum | solution.py:387
  107.0 0.0 copy-done.1
  (7 shorter events, 0.0 us)
Async XLA Ops:
  0.0 5.4 %copy-start = (s32[256,128]{1,0:T(8,128)S(1)}, s32[256,128]{1,0:T(8,128)}, u32[]{:S(2)}) copy-start(s32[256,128]{1,0:T(8,128)} %param.13) | copy-start | bytes 393220
  1.3 35.2 %collective-permute-start.2 = (bf16[2048,128]{1,0:T(8,128)(2,1)S(1)}, bf16[2048,128]{1,0:T(8,128)(2,1)S(1)}, u32[]{:S(2)}, u32[]{:S(2)}) collective-permute-start(bf16[2048,128]{1,0:T(8,128)(2,1)S(1)} %bitcast.35), channel_id=1, source_target_pairs={{0,24},{8,0},{16,8},{24,16},{1,25},{9,1},{17,9},{25,17},{2,26},{10... | collective-permute-start | bytes 1572872 | tf_op jit(solution)/shard_map/ppermute | solution.py:332
  3.7 32.7 %collective-permute-start.1 = (bf16[2048,128]{1,0:T(8,128)(2,1)S(1)}, bf16[2048,128]{1,0:T(8,128)(2,1)S(1)}, u32[]{:S(2)}, u32[]{:S(2)}) collective-permute-start(bf16[2048,128]{1,0:T(8,128)(2,1)S(1)} %bitcast.36), channel_id=1, source_target_pairs={{0,16},{8,24},{16,0},{24,8},{1,17},{9,25},{17,1},{25,9},{2,18},{10... | collective-permute-start | bytes 1572872 | tf_op jit(solution)/shard_map/ppermute | solution.py:332
  4.4 32.1 %collective-permute-start = (bf16[2048,128]{1,0:T(8,128)(2,1)S(1)}, bf16[2048,128]{1,0:T(8,128)(2,1)S(1)}, u32[]{:S(2)}, u32[]{:S(2)}) collective-permute-start(bf16[2048,128]{1,0:T(8,128)(2,1)S(1)} %bitcast.37), channel_id=1, source_target_pairs={{0,8},{8,16},{16,24},{24,0},{1,9},{9,17},{17,25},{25,1},{2,10},{10... | collective-permute-start | bytes 1572872 | tf_op jit(solution)/shard_map/ppermute | solution.py:332
  36.5 0.8 copy-start.3
  36.5 1.0 copy-start.4
  37.5 1.5 %slice-start = ((s32[8,8,128]{2,1,0:T(8,128)}), s32[8,3,128]{2,1,0:T(4,128)S(1)}, s32[]{:S(2)}) async-start(s32[8,8,128]{2,1,0:T(8,128)} %shard_map.83), calls=%async_computation.2 | async-start | bytes 32768 | tf_op jit(solution)/shard_map/slice | solution.py:361
  39.6 12.9 %copy-start.2 = (bf16[256]{0:T(256)(128)(2,1)S(1)}, bf16[256]{0:T(256)(128)(2,1)}, u32[]{:S(2)}) copy-start(bf16[256]{0:T(256)(128)(2,1)} %param.14) | copy-start | bytes 1540
  46.6 6.7 %copy-start.5 = (s32[8,8,128]{2,1,0:T(8,128)S(1)}, s32[8,8,128]{2,1,0:T(8,128)}, u32[]{:S(2)}) copy-start(s32[8,8,128]{2,1,0:T(8,128)} %shard_map.83) | copy-start | bytes 98308
  46.6 26.3 %all-to-all-start.1 = ((bf16[8,384,128]{2,1,0:T(8,128)(2,1)}), bf16[8,384,128]{2,1,0:T(8,128)(2,1)S(1)}, u32[]{:S(2)}, u32[]{:S(2)}) async-start(bf16[8,384,128]{2,1,0:T(8,128)(2,1)} %bitcast.34), calls=%async_computation.1 | async-start | bytes 1572864 | tf_op jit(solution)/shard_map/all_to_all | solution.py:362
  73.0 32.7 %copy-start.6 = (s32[64,128]{1,0:T(8,128)S(1)}, s32[64,128]{1,0:T(8,128)}, u32[]{:S(2)}) copy-start(s32[64,128]{1,0:T(8,128)} %param.17) | copy-start | bytes 98308
  93.4 13.6 %copy-start.1 = (s32[256,128]{1,0:T(8,128)S(1)}, s32[256,128]{1,0:T(8,128)}, u32[]{:S(2)}) copy-start(s32[256,128]{1,0:T(8,128)} %param.13) | copy-start | bytes 393220
